TPU v7x, 512 devices: a whole 4x4x16 slice. The times are simulated.
512 devices in a mesh: leaf: 128 (over x, z, core), rep: 4 (over y).
Axes of the slice: x: 4, y: 4, z: 16, core: 2. Of those that a mesh axis runs over, the one named last changes fastest.
Arguments:
- coords: bfloat16 [64, 524288], P(None, 'leaf'), may hold values from -1.5 to 1.5
- right_sides: bfloat16 [32, 524288], P('rep', 'leaf'), may hold values from -0.59765625 to 0.59765625
- leaf_order: int32 [524288], P('leaf'), may hold values from 0 to 4095, as said below
- leaf_basis: bfloat16 [2048, 256, 128], P('leaf'), may hold values from -0.375 to 0.375
- leaf_transfer: bfloat16 [2048, 128, 128], P('leaf'), may hold values from -0.5 to 0.5
- top_transfer: bfloat16 [6, 2, 128, 128], replicated, may hold values from -0.375 to 0.375
- skel_leaf: int32 [2048, 128], P('leaf'), may hold values from 0 to 255, as said below
- skel_root: int32 [128, 128], P('leaf'), may hold values from 0 to 4095, as said below
- admissible: int32 [2048, 8], P('leaf'), may hold values from 0 to 15, as said below
- near_leaves: int32 [2048, 24], P('leaf'), may hold values from 0 to 47, as said below
- near_count: int32 [2048], P('leaf'), may hold values from 2 to 24, as said below
Outputs:
- applied: float32 [32, 524288], P('rep', 'leaf')
Inputs may be any that keep to these rules, and one draw needn't show every extreme that they name: `leaf_order`: each subtree's block of 4096 entries is a permutation. `skel_leaf`: each row holds 128 distinct positions. `skel_root`: each row holds 128 distinct positions. `admissible`: never the row's own leaf; entries may repeat. `near_leaves`: entries 0 to 15 are leaves of the previous subtree, the next 16 those of the own one, the last 16 those of the next one; slot 0 is the leaf itself; the first subtree never names the previous one and the last never the next; entries may repeat; only the first near_count entries of a row are live. `near_count`: leaf 0 has all 24 slots live.
All inputs are finite; a program needn't handle non-finite values.
Results may differ from a plain program's by a relative error of at most 0.0029.
Values may be sent and summed in bfloat16 or wider, within the bound.
A program may use at most 64 MiB of HBM per device.

v0:
```python
import functools

import jax
import jax.numpy as jnp
from jax import lax
from jax.experimental import pallas as pl
from jax.experimental.pallas import tpu as pltpu
from jax.sharding import PartitionSpec as P

MESH = pl.DeviceIdType.MESH
F32 = jnp.float32
BF16 = jnp.bfloat16
I32 = jnp.int32

DIM = 64
RANK = 128
LEAF = 256
LEAVES = 16
PTS = 4096
LANES = 128
BLOCKS = PTS // LANES
REPS = 4
QUARTER = LEAVES // REPS
OWN = 8
RHS = 32
SIDES = 3
PARTNERS = SIDES * QUARTER
PHASES = (3, 2, 2)
WAYS = 2
CHUNKS = 4
VMEM_LIMIT = 24 * 1024 * 1024


def dot_nn(a, b):
    return lax.dot_general(a, b, (((1,), (0,)), ((), ())), preferred_element_type=F32)


def dot_nt(a, b):
    return lax.dot_general(a, b, (((1,), (1,)), ((), ())), preferred_element_type=F32)


def kernel_values(shifted):
    shifted = jnp.maximum(shifted, 1.0)
    return jnp.exp((shifted * -0.5) * lax.rsqrt(shifted))


def split_two(x):
    high = x.astype(BF16)
    return high, (x - high.astype(F32)).astype(BF16)


def stack_two(x):
    high = x.astype(BF16).astype(F32)
    return jnp.concatenate([high, x - high], axis=0).astype(BF16)


def fold_two(x):
    half = x.shape[0] // 2
    return x[:half] + x[half:]


def dot_wide(x, matrix):
    return fold_two(dot_nn(stack_two(x), matrix))


def dot_wide_nt(x, matrix):
    return fold_two(dot_nt(stack_two(x), matrix))


def dot_both_wide(x, matrix):
    rows = stack_two(x)
    high, low = split_two(matrix)
    return fold_two(dot_nn(rows, high)) + fold_two(dot_nn(rows, low))


def with_norms(points, own):
    count = points.shape[1]
    norm = jnp.sum(points * points, axis=0, keepdims=True)
    if own:
        norm = norm + 1.0
    high = norm.astype(BF16).astype(F32)
    rest = norm - high
    mid = rest.astype(BF16).astype(F32)
    low = rest - mid
    row = lax.broadcasted_iota(I32, (16, count), 0)
    if not own:
        row = row - 3
    tail = jnp.where(row == 0, high, jnp.where(row == 1, mid, jnp.where(row == 2, low, 0.0)))
    ones = lax.broadcasted_iota(I32, (16, count), 0) - (3 if own else 0)
    tail = jnp.where((ones >= 0) & (ones < 3), 1.0, tail)
    head = points * -2.0 if own else points
    return jnp.concatenate([head, tail, jnp.zeros((LANES - DIM - 16, count), F32)], axis=0)


def one_hot(low):
    row = lax.broadcasted_iota(I32, (LEAF, low.shape[1]), 0)
    return jnp.where(row == low, 1.0, 0.0).astype(BF16)


def choose(slices, positions):
    marks = one_hot(positions & 255)
    rows = slices[0].shape[0]
    high = jnp.broadcast_to(positions >> 8, (rows, positions.shape[1]))
    out = jnp.zeros((rows, positions.shape[1]), F32)
    together = min(len(slices), 512 // rows)
    for first in range(0, len(slices), together):
        block = dot_nn(jnp.concatenate(slices[first : first + together], axis=0), marks)
        for number in range(together):
            out = jnp.where(high == first + number, block[number * rows : (number + 1) * rows], out)
    return out


def order_of(order_ref, leaf):
    return jnp.concatenate([order_ref[pl.ds(leaf * 2 + half, 1), :] for half in range(2)], axis=1)


def pick(table, lanes):
    return jnp.take_along_axis(table, lanes, axis=1, mode="promise_in_bounds")


def greet_signals(devices):
    barrier = pltpu.get_barrier_semaphore()
    for device in devices:
        pl.semaphore_signal(barrier, inc=1, device_id=device, device_id_type=MESH)


def greet_wait(devices):
    pl.semaphore_wait(pltpu.get_barrier_semaphore(), len(devices))


def remote(source, target, send_sem, recv_sem, device):
    return pltpu.make_async_remote_copy(
        src_ref=source,
        dst_ref=target,
        send_sem=send_sem,
        recv_sem=recv_sem,
        device_id=device,
        device_id_type=MESH,
    )


def phases_of(levels):
    spans, first = [], 0
    for width in PHASES:
        width = min(width, levels - first)
        if width > 0:
            spans.append((first, width))
        first += width
    return spans


def vectors_kernel(rows_ref, order_ref, sorted_ref):
    vector_rows = rows_ref[...]

    def sort_vectors(number, _):
        positions = order_of(order_ref, number)
        block = dot_nn(vector_rows, one_hot(positions & 255))
        high = jnp.broadcast_to(positions >> 8, (OWN, LEAF))
        out = jnp.zeros((OWN, LEAF), F32)
        for source in range(LEAVES):
            out = jnp.where(high == source, block[source * OWN : (source + 1) * OWN], out)
        sorted_ref[number] = out
        return 0

    lax.fori_loop(0, LEAVES, sort_vectors, 0, unroll=4)


def gather_kernel(
    count,
    levels,
    coords_ref,
    sorted_ref,
    order_ref,
    basis_ref,
    transfer_ref,
    top_ref,
    skel_root_ref,
    skel_leaf_ref,
    admissible_ref,
    near_ref,
    count_ref,
    window_ref,
    columns_ref,
    window_vectors_ref,
    t_root_ref,
    times_ref,
    skel_out_ref,
    vectors_ref,
    points_ref,
    got_points_ref,
    kernel_ref,
    sibling_ref,
    *rest,
):
    spans = phases_of(levels)
    gathered_refs = rest[: len(spans)]
    spread_sems = rest[len(spans) : 2 * len(spans)]
    row_sems, column_sems, vector_sems, push_sems = rest[2 * len(spans) :]

    leaf = lax.axis_index("leaf")
    rep = lax.axis_index("rep")
    before = lax.rem(leaf + count - 1, count)
    after = lax.rem(leaf + 1, count)
    others = [lax.rem(rep + step, REPS) for step in range(1, REPS)]
    partners = [(side, other) for side in (before, after) for other in [rep] + others]
    partners += [(leaf, other) for other in others]
    for first, width in spans:
        partners += [(leaf ^ (number << first), rep) for number in range(1, 1 << width)]
    greet_signals(partners)

    def coordinate_slices():
        return [coords_ref[:, high * LEAF : (high + 1) * LEAF] for high in range(LEAVES)]

    at = jnp.broadcast_to(skel_root_ref[...], (8, LANES))
    at_high = at >> 7
    at_low = at & 127
    initial = jnp.zeros((8, LANES), I32)
    for source in range(BLOCKS):
        table = jnp.broadcast_to(order_ref[source : source + 1, :], (8, LANES))
        initial = jnp.where(at_high == source, pick(table, at_low), initial)
    points_ref[0] = choose(coordinate_slices(), initial[:1]).astype(BF16)
    sent = []

    pushes = [[] for _ in spans]

    def push_start(phase):
        if phase >= len(spans):
            return
        first, width = spans[phase]
        for level in range(first, first + width):
            for number in range(1 << (level - first), 2 << (level - first)):
                copy = remote(
                    points_ref.at[first],
                    got_points_ref.at[level],
                    push_sems.at[0, level, number - (1 << (level - first))],
                    push_sems.at[1, level, 0],
                    (leaf ^ (number << first), rep),
                )
                pushes[phase].append((level, copy))
                if level == first:
                    copy.start()
                else:
                    pl.when(lax.rem(leaf // (1 << first), 1 << (level - first)) == 0)(copy.start)

    def push_finish(phase):
        if phase >= len(spans):
            return
        first, width = spans[phase]
        for level in range(first, first + width):
            [copy for at, copy in pushes[phase] if at == level][0].wait_recv()
            if level + 1 < levels:
                on_right = lax.rem(leaf // (1 << level), 2) == 1
                points_ref[level + 1] = jnp.where(
                    on_right, got_points_ref[level].astype(F32), points_ref[level].astype(F32)
                ).astype(BF16)
        push_start(phase + 1)

    def push_wait_send():
        for (first, width), copies in zip(spans, pushes):
            for level, copy in copies:
                if level == first:
                    copy.wait_send()
                else:
                    pl.when(lax.rem(leaf // (1 << first), 1 << (level - first)) == 0)(copy.wait_send)

    def kernels(first, last):
        first, last = min(first, levels), min(last, levels)
        values = []
        for level in range(first, last):
            own = with_norms(points_ref[level].astype(F32), True).astype(BF16)
            rows = with_norms(got_points_ref[level].astype(F32), False).T.astype(BF16)
            values.append(split_two(kernel_values(dot_nn(rows, own))))
        for level, (high, low) in zip(range(first, last), values):
            kernel_ref[level, 0] = high
            kernel_ref[level, 1] = low

    spreads = []

    def spread_start(phase):
        if phase >= len(spans):
            return
        first, width = spans[phase]
        copies = []
        for number in range(1, 1 << width):
            copy = remote(
                gathered_refs[phase].at[0],
                gathered_refs[phase].at[number],
                spread_sems[phase].at[0, number],
                spread_sems[phase].at[1, number],
                (leaf ^ (number << first), rep),
            )
            copy.start()
            copies.append(copy)
            sent.append(copy)
        spreads.append(copies)

    def spread_finish(phase):
        if phase >= len(spans):
            return
        first, width = spans[phase]
        for copy in spreads[phase]:
            copy.wait_recv()
        nodes = [gathered_refs[phase][number] for number in range(1 << width)]
        for level in range(first, first + width):
            sibling_ref[level] = nodes[1]
            if level + 1 == levels:
                return
            on_right = lax.rem(leaf // (1 << level), 2) == 1
            even = jnp.concatenate(nodes[0::2], axis=0)
            odd = jnp.concatenate(nodes[1::2], axis=0)
            parents = dot_wide(jnp.where(on_right, odd, even), top_ref[level, 0]) + dot_wide(
                jnp.where(on_right, even, odd), top_ref[level, 1]
            )
            nodes = [parents[i * OWN : i * OWN + OWN] for i in range(len(nodes) // 2)]
        gathered_refs[phase + 1][0] = nodes[0]
        spread_start(phase + 1)

    def coupling(level):
        rows = stack_two(sibling_ref[level])
        return fold_two(dot_nn(rows, kernel_ref[level, 0])) + fold_two(dot_nn(rows, kernel_ref[level, 1]))

    def up(number, total):
        s_leaf = dot_nn(sorted_ref[number].astype(BF16), basis_ref[number])
        return total + dot_nn(stack_two(s_leaf), transfer_ref[number])

    s_root = fold_two(lax.fori_loop(0, LEAVES, up, jnp.zeros((2 * OWN, RANK), F32), unroll=LEAVES))
    gathered_refs[0][0] = s_root
    greet_wait(partners)
    spread_start(0)
    push_start(0)

    for target in range(REPS):
        for column in range(2):
            top = sorted_ref[column * REPS + target]
            bottom = sorted_ref[(column + 2) * REPS + target]
            vectors_ref[target, :, column * LEAF : (column + 1) * LEAF] = jnp.concatenate(
                [top, bottom], axis=0
            ).astype(BF16)
    window_vectors_ref[1, rep] = vectors_ref[rep]
    vector_moves = [
        (index, side, device, step)
        for index, (side, device) in enumerate(((2, before), (0, after), (1, leaf)))
        for step in range(REPS)
        if side != 1 or step > 0
    ]
    for index, side, device, step in vector_moves:
        target = lax.rem(rep + step, REPS)
        copy = remote(
            vectors_ref.at[target],
            window_vectors_ref.at[side, rep],
            vector_sems.at[0, index, step],
            vector_sems.at[1, index, step],
            (device, target),
        )
        copy.start()
        sent.append(copy)

    row_copies = []

    def sort_points(k):
        number = k * REPS + rep
        points = choose(coordinate_slices(), order_of(order_ref, number))
        columns_ref[rep, k] = points.astype(BF16)
        window_ref[1, k] = with_norms(points, False).T.astype(BF16)

    def send_points(pair):
        span = pl.ds(pair * 2, 2)
        for index, (side, device) in enumerate(((2, before), (0, after))):
            copy = remote(
                window_ref.at[1, span],
                window_ref.at[side, span],
                row_sems.at[0, pair, index],
                row_sems.at[1, pair, index],
                (device, rep),
            )
            copy.start()
            row_copies.append(copy)
            sent.append(copy)
        for step, other in enumerate(others):
            copy = remote(
                columns_ref.at[rep, span],
                columns_ref.at[rep, span],
                column_sems.at[0, pair, step],
                column_sems.at[1, pair, step],
                (leaf, other),
            )
            copy.start()
            sent.append(copy)

    sort_points(0)
    sort_points(1)
    send_points(0)
    push_finish(0)
    spread_finish(0)
    sort_points(2)
    sort_points(3)
    send_points(1)
    push_finish(1)
    spread_finish(1)
    kernels(0, 5)
    push_finish(2)
    kernels(5, 7)

    diagonal = lax.broadcasted_iota(I32, (LEAVES, LEAVES), 0) == lax.broadcasted_iota(
        I32, (LEAVES, LEAVES), 1
    )

    def as_column(row):
        return jnp.sum(jnp.where(diagonal, row, 0.0), axis=1, keepdims=True)

    near = near_ref[...]
    slot = lax.broadcasted_iota(I32, near.shape, 1)
    live = slot.astype(F32) < as_column(count_ref[...].astype(F32))
    admissible = admissible_ref[...]
    lane = lax.broadcasted_iota(I32, (LEAVES, LANES), 1)
    times = jnp.zeros((LEAVES, LANES), F32)
    for entry in range(PARTNERS + QUARTER):
        if entry < PARTNERS:
            named = jnp.where(near == entry * REPS + rep, 1.0, 0.0)
            total = jnp.sum(jnp.where(live, named, 0.0), axis=1, keepdims=True)
        else:
            named = jnp.where(admissible == (entry - PARTNERS) * REPS + rep, 1.0, 0.0)
            total = as_column(jnp.sum(named, axis=0, keepdims=True))
        times = jnp.where(lane == entry, total, times)
    times_ref[...] = times.astype(I32)
    skel_out_ref[...] = skel_leaf_ref[...]

    spread_finish(2)

    running = coupling(levels - 1)
    for level in range(levels - 2, -1, -1):
        side = lax.rem(leaf // (1 << level), 2)
        running = coupling(level) + dot_wide_nt(running, top_ref[level, side])
    t_root_ref[...] = running

    for copy in row_copies:
        copy.wait_recv()
    for pair in range(2):
        span = pl.ds(pair * 2, 2)
        for step, other in enumerate(others):
            source = lax.rem(rep + REPS - 1 - step, REPS)
            remote(
                columns_ref.at[rep, span],
                columns_ref.at[source, span],
                column_sems.at[0, pair, step],
                column_sems.at[1, pair, step],
                (leaf, other),
            ).wait_recv()
    for index, side, device, step in vector_moves:
        source = lax.rem(rep + REPS - step, REPS)
        remote(
            vectors_ref.at[rep],
            window_vectors_ref.at[side, source],
            vector_sems.at[0, index, step],
            vector_sems.at[1, index, step],
            (device, lax.rem(rep + step, REPS)),
        ).wait_recv()
    for copy in sent:
        copy.wait_send()
    push_wait_send()


def near_kernel(
    times_ref,
    columns_ref,
    skel_leaf_ref,
    t_root_ref,
    window_vectors_ref,
    transfer_ref,
    basis_ref,
    window_ref,
    out_ref,
    own_out_ref,
    list_ref,
    own_ref,
    own_skel_ref,
    skel_rows_ref,
    vectors_ref,
    total_ref,
    s_ref,
    t_ref,
    near_shifted_even,
    near_shifted_odd,
    near_even,
    near_odd,
    far_shifted_even,
    far_shifted_odd,
    far_even,
    far_odd,
):
    near_shifted, near_tiles = (near_shifted_even, near_shifted_odd), (near_even, near_odd)
    far_shifted, far_tiles = (far_shifted_even, far_shifted_odd), (far_even, far_odd)
    rep = lax.axis_index("rep")
    root_rows = stack_two(t_root_ref[...])
    t_ref[...] = jnp.zeros_like(t_ref)

    def prepare(leaf, _):
        source = lax.rem(leaf, REPS)
        k = leaf // REPS
        points = columns_ref[source, k].astype(F32)
        columns = with_norms(points, True)
        own_ref[leaf] = columns.astype(BF16)
        marks = one_hot(skel_leaf_ref[pl.ds(leaf, 1), :])
        own_skel_ref[leaf] = with_norms(dot_nn(columns_ref[source, k], marks), True).astype(BF16)
        return 0

    lax.fori_loop(0, LEAVES, prepare, 0, unroll=4)

    def from_root(leaf, _):
        t_ref[leaf, pl.ds(pl.multiple_of(rep * OWN, OWN), OWN), :] = fold_two(
            dot_nt(root_rows, transfer_ref[leaf])
        )
        return 0

    lax.fori_loop(0, LEAVES, from_root, 0, unroll=8)

    for side in range(SIDES):
        for column in range(2):
            span = slice(column * LEAF, (column + 1) * LEAF)
            blocks = [window_vectors_ref[side, source, :, span].astype(F32) for source in range(REPS)]
            vectors_ref[side * QUARTER + column] = jnp.concatenate(
                [block[:OWN] for block in blocks], axis=0
            ).astype(BF16)
            vectors_ref[side * QUARTER + column + 2] = jnp.concatenate(
                [block[OWN:] for block in blocks], axis=0
            ).astype(BF16)
    for k in range(QUARTER):
        leaf = k * REPS + rep
        s_leaf = dot_nn(vectors_ref[QUARTER + k], basis_ref[leaf])
        s_ref[k] = stack_two(s_leaf)
        skel = own_skel_ref[leaf].astype(F32)
        skel_rows_ref[k] = with_norms(skel[:DIM] * -0.5, False).T.astype(BF16)

    total_ref[...] = jnp.zeros_like(total_ref)

    def make_list(first, width):
        def one_leaf(leaf, filled):
            for entry in range(first, first + width):
                list_ref[filled] = leaf * 16 + entry
                filled = filled + jnp.where(times_ref[leaf, entry] > 0, 1, 0)
            return filled

        filled = lax.fori_loop(0, LEAVES, one_leaf, 0, unroll=2)
        for pad in range(4 * WAYS):
            list_ref[filled + pad] = first
        return filled

    def run(filled, product, keep, apply, shifted_refs, tile_refs):
        def start(group, shifted_ref):
            for way in range(WAYS):
                code = list_ref[group * WAYS + way]
                shifted_ref[way] = product(code >> 4, code & 15)

        def middle(shifted_ref, tile_ref):
            for way in range(WAYS):
                keep(tile_ref, way, kernel_values(shifted_ref[way]))

        def finish(group, tile_ref):
            for way in range(WAYS):
                number = group * WAYS + way
                code = list_ref[jnp.maximum(number, 0)]
                leaf, entry = code >> 4, code & 15
                times = jnp.where((number >= 0) & (number < filled), times_ref[leaf, entry], 0)
                apply(leaf, entry, times.astype(F32), tile_ref, way)

        start(0, shifted_refs[0])
        tile_refs[1][...] = jnp.zeros_like(tile_refs[1])

        def step(number, _):
            even = number * 2
            start(even + 1, shifted_refs[1])
            middle(shifted_refs[0], tile_refs[0])
            finish(even - 1, tile_refs[1])
            start(even + 2, shifted_refs[0])
            middle(shifted_refs[1], tile_refs[1])
            finish(even, tile_refs[0])
            return 0

        steps = (filled + 2 * WAYS - 1) // (2 * WAYS)
        lax.fori_loop(0, steps, step, 0)
        finish(2 * steps - 1, tile_refs[1])

    def near_keep(tile_ref, way, values):
        tile_ref[way] = values.astype(BF16)

    def near_apply(leaf, entry, times, tile_ref, way):
        total_ref[leaf] += dot_nn(vectors_ref[entry], tile_ref[way]) * times

    run(
        make_list(0, PARTNERS),
        lambda leaf, entry: dot_nn(window_ref[entry], own_ref[leaf]),
        near_keep,
        near_apply,
        near_shifted,
        near_tiles,
    )

    def far_keep(tile_ref, way, values):
        high, low = split_two(values)
        tile_ref[way, 0] = high
        tile_ref[way, 1] = low

    def far_apply(leaf, entry, times, tile_ref, way):
        rows = s_ref[entry - PARTNERS]
        term = fold_two(dot_nn(rows, tile_ref[way, 0])) + dot_nn(rows[:RHS], tile_ref[way, 1])
        t_ref[leaf] += term * times

    run(
        make_list(PARTNERS, QUARTER),
        lambda leaf, entry: dot_nn(skel_rows_ref[entry - PARTNERS], own_skel_ref[leaf]),
        far_keep,
        far_apply,
        far_shifted,
        far_tiles,
    )

    for leaf in range(LEAVES):
        total_ref[leaf] += dot_wide_nt(t_ref[leaf], basis_ref[leaf])
    mine = pl.ds(pl.multiple_of(rep * OWN, OWN), OWN)
    for leaf in range(LEAVES):
        own_out_ref[:, leaf * LEAF : (leaf + 1) * LEAF] = total_ref[leaf, mine, :]
    for leaf in range(LEAVES // 2):
        top = total_ref[leaf].reshape(REPS, OWN, LEAF)
        bottom = total_ref[leaf + LEAVES // 2].reshape(REPS, OWN, LEAF)
        out_ref[:, :, leaf * LEAF : (leaf + 1) * LEAF] = jnp.concatenate([top, bottom], axis=1).astype(BF16)


def combine_kernel(part_ref, own_ref, order_ref, out_ref, got_ref, sems):
    leaf = lax.axis_index("leaf")
    rep = lax.axis_index("rep")
    half = PTS // 2
    width = half // CHUNKS
    partners = [(leaf, lax.rem(rep + step, REPS)) for step in range(1, REPS)]
    greet_signals(partners)
    greet_wait(partners)
    copies = []
    for chunk in range(CHUNKS):
        span = pl.ds(chunk * width, width)
        for index, partner in enumerate(partners):
            copy = remote(
                part_ref.at[partner[1], :, span],
                got_ref.at[index, :, span],
                sems.at[0, index, chunk],
                sems.at[1, index, chunk],
                partner,
            )
            copy.start()
            copies.append(copy)

    scattered = jnp.zeros((LEAVES * 2 * OWN, LEAF), F32)
    for chunk in range(CHUNKS):
        here = [(number, (number * half + chunk * width) // LANES) for number in range(2)]
        positions = jnp.concatenate(
            [
                order_ref[first + at : first + at + 1, :]
                for _, first in here
                for at in range(width // LANES)
            ],
            axis=1,
        )
        marks = one_hot(positions & 255)
        high = jnp.broadcast_to(positions >> 8, (2 * OWN, 2 * width))
        for copy in copies[chunk * len(partners) : (chunk + 1) * len(partners)]:
            copy.wait_recv()
        totals = []
        for number, first in here:
            rows = slice(number * OWN, (number + 1) * OWN)
            total = -own_ref[:, first * LANES : first * LANES + width]
            for index in range(REPS - 1):
                total = total - got_ref[index, :, chunk * width : (chunk + 1) * width].astype(F32)[rows]
            totals.append(total)
        total = jnp.concatenate(totals, axis=1)
        rounded = total.astype(BF16).astype(F32)
        terms = jnp.concatenate([rounded, total - rounded], axis=0)
        rows = jnp.concatenate(
            [jnp.where(high == source, terms, 0.0).astype(BF16) for source in range(LEAVES)], axis=0
        )
        scattered = scattered + dot_nt(rows, marks)
    for source in range(LEAVES):
        first = source * 2 * OWN
        out_ref[:, source * LEAF : (source + 1) * LEAF] = (
            scattered[first : first + OWN] + scattered[first + OWN : first + 2 * OWN]
        )
    for copy in copies:
        copy.wait_send()


def vmem(count):
    return [pl.BlockSpec(memory_space=pltpu.VMEM)] * count


def shape(dims, dtype):
    return jax.ShapeDtypeStruct(dims, dtype)


def params(collective_id=None):
    if collective_id is None:
        return pltpu.CompilerParams(vmem_limit_bytes=VMEM_LIMIT)
    return pltpu.CompilerParams(
        collective_id=collective_id, has_side_effects=True, vmem_limit_bytes=VMEM_LIMIT
    )


def on_device(
    count,
    coords,
    right_sides,
    leaf_order,
    leaf_basis,
    leaf_transfer,
    top_transfer,
    skel_leaf,
    skel_root,
    admissible,
    near_leaves,
    near_count,
):
    levels = count.bit_length() - 1
    spans = phases_of(levels)
    order = leaf_order.reshape(BLOCKS, LANES)
    dma = pltpu.SemaphoreType.DMA
    sorted_vectors = pl.pallas_call(
        vectors_kernel,
        out_shape=shape((LEAVES, OWN, LEAF), F32),
        in_specs=vmem(2),
        out_specs=pl.BlockSpec(memory_space=pltpu.VMEM),
        compiler_params=params(),
        cost_estimate=pl.CostEstimate(flops=10**9, bytes_accessed=10**6, transcendentals=0),
        name="vectors",
    )(
        right_sides.reshape(OWN, LEAVES, LEAF).transpose(1, 0, 2).reshape(LEAVES * OWN, LEAF),
        order,
    )
    window, columns, window_vectors, t_root, times, skel_here = pl.pallas_call(
        functools.partial(gather_kernel, count, levels),
        out_shape=(
            shape((SIDES, QUARTER, LEAF, LANES), BF16),
            shape((REPS, QUARTER, DIM, LEAF), BF16),
            shape((SIDES, REPS, 2 * OWN, 2 * LEAF), BF16),
            shape((OWN, RANK), F32),
            shape((LEAVES, LANES), I32),
            shape((LEAVES, RANK), I32),
        ),
        in_specs=vmem(11),
        out_specs=tuple(vmem(6)),
        scratch_shapes=[
            pltpu.VMEM((REPS, 2 * OWN, 2 * LEAF), BF16),
            pltpu.VMEM((levels, DIM, RANK), BF16),
            pltpu.VMEM((levels, DIM, RANK), BF16),
            pltpu.VMEM((levels, 2, RANK, RANK), BF16),
            pltpu.VMEM((levels, OWN, RANK), F32),
        ]
        + [pltpu.VMEM((1 << width, OWN, RANK), F32) for _, width in spans]
        + [dma((2, 1 << width)) for _, width in spans]
        + [
            dma((2, 2, 2)),
            dma((2, 2, REPS - 1)),
            dma((2, SIDES, REPS)),
            dma((2, levels, 1 << (max(PHASES) - 1))),
        ],
        compiler_params=params(0),
        name="gather",
    )(
        coords,
        sorted_vectors,
        order,
        leaf_basis,
        leaf_transfer,
        top_transfer[: levels - 1],
        skel_root,
        skel_leaf,
        admissible.T,
        near_leaves,
        near_count.reshape(1, LEAVES),
    )

    part, own_part = pl.pallas_call(
        near_kernel,
        out_shape=(shape((REPS, 2 * OWN, PTS // 2), BF16), shape((OWN, PTS), F32)),
        in_specs=[pl.BlockSpec(memory_space=pltpu.SMEM)] + vmem(7),
        out_specs=tuple(vmem(2)),
        scratch_shapes=[
            pltpu.SMEM((LEAVES * PARTNERS + 4 * WAYS + 8,), I32),
            pltpu.VMEM((LEAVES, LANES, LEAF), BF16),
            pltpu.VMEM((LEAVES, LANES, RANK), BF16),
            pltpu.VMEM((QUARTER, RANK, LANES), BF16),
            pltpu.VMEM((PARTNERS, RHS, LEAF), BF16),
            pltpu.VMEM((LEAVES, RHS, LEAF), F32),
            pltpu.VMEM((QUARTER, 2 * RHS, RANK), BF16),
            pltpu.VMEM((LEAVES, RHS, RANK), F32),
        ]
        + [pltpu.VMEM((WAYS, LEAF, LEAF), F32)] * 2
        + [pltpu.VMEM((WAYS, LEAF, LEAF), BF16)] * 2
        + [pltpu.VMEM((WAYS, RANK, RANK), F32)] * 2
        + [pltpu.VMEM((WAYS, 2, RANK, RANK), BF16)] * 2,
        compiler_params=params(),
        name="near",
    )(
        times,
        columns,
        skel_here,
        t_root,
        window_vectors,
        leaf_transfer,
        leaf_basis,
        window.reshape(PARTNERS, LEAF, LANES),
    )

    negative = pl.pallas_call(
        combine_kernel,
        out_shape=shape((OWN, PTS), F32),
        in_specs=vmem(3),
        out_specs=pl.BlockSpec(memory_space=pltpu.VMEM),
        scratch_shapes=[
            pltpu.VMEM((REPS - 1, 2 * OWN, PTS // 2), BF16),
            dma((2, REPS - 1, CHUNKS)),
        ],
        compiler_params=params(1),
        name="combine",
    )(part, own_part, order)
    return -negative


def solution(mesh):
    placed = (
        P(None, "leaf"),
        P("rep", "leaf"),
        P("leaf"),
        P("leaf", None, None),
        P("leaf", None, None),
        P(),
        P("leaf", None),
        P("leaf", None),
        P("leaf", None),
        P("leaf", None),
        P("leaf"),
    )
    return jax.shard_map(
        functools.partial(on_device, mesh.shape["leaf"]),
        mesh=mesh,
        in_specs=placed,
        out_specs=P("rep", "leaf"),
        check_vma=False,
    )
```

profile of v0, /device:TPU:2, one launch (start us, length us, event | category | flops | bytes accessed | tf_op | source)
XLA Modules:
  0.0 54.7 jit_solution(17219942575724820028)
XLA Ops:
  0.0 0.0 copy-start.4
  0.0 0.7 %copy-done.4 = s32[4096]{0:T(1024)S(1)} copy-done((s32[4096]{0:T(1024)S(1)}, s32[4096]{0:T(1024)}, u32[]{:S(2)}) %copy-start.4) | copy-done | bytes 16408
  0.7 0.0 copy-start.11
  0.7 0.8 %copy-done.11 = bf16[8,4096]{1,0:T(8,128)(2,1)S(1)} copy-done((bf16[8,4096]{1,0:T(8,128)(2,1)S(1)}, bf16[8,4096]{1,0:T(8,128)(2,1)}, u32[]{:S(2)}) %copy-start.11) | copy-done | bytes 65560
  1.6 0.0 copy-start
  1.6 0.0 copy-start.1
  1.6 0.0 copy-start.2
  1.6 0.0 copy-start.3
  1.6 0.0 copy-start.5
  1.6 0.0 copy-start.6
  1.6 0.0 copy-start.7
  1.6 0.0 copy-start.8
  1.6 0.0 copy-start.9
  1.6 0.0 copy-start.10
  1.6 1.0 %vectors.1.sorted_ref = f32[16,8,256]{2,1,0:T(8,128)S(1)} custom-call(bf16[128,256]{1,0:T(8,128)(2,1)S(1)} %bitcast.15, s32[32,128]{1,0:T(8,128)S(1)} %bitcast.10), custom_call_target="tpu_custom_call" | custom-call | flops 1000000000 | bytes 1000000 | tf_op jit(solution)/shard_map/vectors/pallas_call | solution.py:722
  2.6 0.2 copy-done
  2.8 0.1 copy-done.1
  2.9 0.2 copy-done.2
  3.1 0.1 copy-done.3
  3.2 0.0 copy-done.5
  3.2 0.0 copy-done.6
  3.2 0.0 copy-done.7
  3.2 0.0 copy-done.8
  3.2 0.0 copy-done.9
  3.2 0.0 copy-done.10
  3.2 30.2 %gather.1 = (bf16[3,4,256,128]{3,2,1,0:T(8,128)(2,1)S(1)}, bf16[4,4,64,256]{3,2,1,0:T(8,128)(2,1)S(1)}, bf16[3,4,16,512]{3,2,1,0:T(8,128)(2,1)S(1)}, f32[8,128]{...) custom-call(bf16[64,4096]{1,0:T(8,128)(2,1)S(1)} %copy-done.2, f32[16,8,256]{2,1,0:T(8,128)S(1)} %vectors.1.sorted_ref, ...), custom_call_target="tpu_custom_call" | custom-call | tf_op jit(solution)/shard_map/gather/pallas_call | solution.py:734
  33.4 10.1 %near.1 = (bf16[4,16,2048]{2,1,0:T(8,128)(2,1)S(1)}, f32[8,4096]{1,0:T(8,128)S(1)}) custom-call(s32[16,128]{1,0:T(8,128)S(1)} %get-tuple-element.13.times_ref, bf16[4,4,64,256]{3,2,1,0:T(8,128)(2,1)S(1)} %get-tuple-element.14.columns_ref, s32[16,128]{1,0:T(8,128)S(1)} %get-tuple-element.15.skel_leaf_ref, f32[8,128]{1,0:T(8,128)S(1)} %get-tuple-element.16.t_root_ref, ...), custom_call_target="tpu_custom_call" | custom-call | tf_op jit(solution)/shard_map/near/pallas_call | solution.py:777
  43.5 10.5 %combine.1 = f32[8,4096]{1,0:T(8,128)S(1)} custom-call(bf16[4,16,2048]{2,1,0:T(8,128)(2,1)S(1)} %get-tuple-element.19.part_ref, f32[8,4096]{1,0:T(8,128)S(1)} %get-tuple-element.20.own_ref, s32[32,128]{1,0:T(8,128)S(1)} %bitcast.12), custom_call_target="tpu_custom_call" | custom-call | tf_op jit(solution)/shard_map/combine/pallas_call | solution.py:809
  54.1 0.7 %neg.3 = f32[8,4096]{1,0:T(8,128)} negate(f32[8,4096]{1,0:T(8,128)S(1)} %combine.1) | non-fusion elementwise | flops 32768 | bytes 262144 | tf_op jit(solution)/shard_map/neg | solution.py:821
Async XLA Ops:
  0.0 0.7 %copy-start.4 = (s32[4096]{0:T(1024)S(1)}, s32[4096]{0:T(1024)}, u32[]{:S(2)}) copy-start(s32[4096]{0:T(1024)} %param.13) | copy-start | bytes 49156
  0.7 0.8 %copy-start.11 = (bf16[8,4096]{1,0:T(8,128)(2,1)S(1)}, bf16[8,4096]{1,0:T(8,128)(2,1)}, u32[]{:S(2)}) copy-start(bf16[8,4096]{1,0:T(8,128)(2,1)} %param.12) | copy-start | bytes 196612
  1.6 1.2 %copy-start = (bf16[16,256,128]{2,1,0:T(8,128)(2,1)S(1)}, bf16[16,256,128]{2,1,0:T(8,128)(2,1)}, u32[]{:S(2)}) copy-start(bf16[16,256,128]{2,1,0:T(8,128)(2,1)} %basis_ref.3) | copy-start | bytes 3145732
  1.6 1.4 %copy-start.1 = (bf16[16,128,128]{2,1,0:T(8,128)(2,1)S(1)}, bf16[16,128,128]{2,1,0:T(8,128)(2,1)}, u32[]{:S(2)}) copy-start(bf16[16,128,128]{2,1,0:T(8,128)(2,1)} %transfer_ref.3) | copy-start | bytes 1572868
  1.6 1.5 %copy-start.2 = (bf16[64,4096]{1,0:T(8,128)(2,1)S(1)}, bf16[64,4096]{1,0:T(8,128)(2,1)}, u32[]{:S(2)}) copy-start(bf16[64,4096]{1,0:T(8,128)(2,1)} %coords_ref.1) | copy-start | bytes 1572868
  1.6 1.6 %copy-start.3 = (bf16[6,2,128,128]{3,2,1,0:T(8,128)(2,1)S(1)}, bf16[6,2,128,128]{3,2,1,0:T(8,128)(2,1)}, u32[]{:S(2)}) copy-start(bf16[6,2,128,128]{3,2,1,0:T(8,128)(2,1)} %top_ref.1) | copy-start | bytes 1179652
  1.6 1.6 %copy-start.5 = (s32[4096]{0:T(1024)S(1)}, s32[4096]{0:T(1024)}, u32[]{:S(2)}) copy-start(s32[4096]{0:T(1024)} %param.13) | copy-start | bytes 49156
  1.6 1.6 %copy-start.6 = (s32[16,128]{1,0:T(8,128)S(1)}, s32[16,128]{1,0:T(8,128)}, u32[]{:S(2)}) copy-start(s32[16,128]{1,0:T(8,128)} %skel_leaf_ref.1) | copy-start | bytes 24580
  1.6 1.6 %copy-start.7 = (s32[16,24]{1,0:T(8,128)S(1)}, s32[16,24]{1,0:T(8,128)}, u32[]{:S(2)}) copy-start(s32[16,24]{1,0:T(8,128)} %near_ref.1) | copy-start | bytes 4612
  1.6 1.6 %copy-start.8 = (s32[16,8]{0,1:T(8,128)S(1)}, s32[16,8]{0,1:T(8,128)}, u32[]{:S(2)}) copy-start(s32[16,8]{0,1:T(8,128)} %param.19) | copy-start | bytes 1540
  1.6 1.6 %copy-start.9 = (s32[1,128]{1,0:T(1,128)S(1)}, s32[1,128]{1,0:T(1,128)}, u32[]{:S(2)}) copy-start(s32[1,128]{1,0:T(1,128)} %skel_root_ref.1) | copy-start | bytes 1540
  1.6 1.6 %copy-start.10 = (s32[16]{0:T(128)S(1)}, s32[16]{0:T(128)}, u32[]{:S(2)}) copy-start(s32[16]{0:T(128)} %param.21) | copy-start | bytes 196
where the time goes:
time: 55 us; the launch traced here: 54.7 us
  Pallas kernels  51.8 us (94%)
  local copies, waits for them, and re-layouts  2.17 us (4%)
  other arithmetic  0.67 us (1%)
    pallas_call x1, Pallas kernels, on_device(): pl.pallas_call(functools.partial(gather_kernel, count, levels), out_shape...  30.2 us
    pallas_call x1, Pallas kernels, on_device(): pl.pallas_call(combine_kernel, out_shape=shape((OWN, PTS), F32), in_specs...  10.5 us
    pallas_call x1, Pallas kernels, on_device(): pl.pallas_call(near_kernel, out_shape=(shape((REPS, 2 * OWN, PTS // 2), B...  10.1 us
    unnamed x24, local copies, waits for them, and re-layouts  2.17 us

commit v1 on v0

--- a/solution.py
+++ b/solution.py
@@ -179,7 +179,7 @@
     admissible_ref,
     near_ref,
     count_ref,
-    window_ref,
+    halo_ref,
     columns_ref,
     window_vectors_ref,
     t_root_ref,
@@ -202,7 +202,7 @@
     before = lax.rem(leaf + count - 1, count)
     after = lax.rem(leaf + 1, count)
     others = [lax.rem(rep + step, REPS) for step in range(1, REPS)]
-    partners = [(side, other) for side in (before, after) for other in [rep] + others]
+    partners = [(jnp.where(lax.rem(leaf, 2) == 0, before, after), rep)]
     partners += [(leaf, other) for other in others]
     for first, width in spans:
         partners += [(leaf ^ (number << first), rep) for number in range(1, 1 << width)]
@@ -337,64 +337,76 @@
                 [top, bottom], axis=0
             ).astype(BF16)
     window_vectors_ref[1, rep] = vectors_ref[rep]
-    vector_moves = [
-        (index, side, device, step)
-        for index, (side, device) in enumerate(((2, before), (0, after), (1, leaf)))
-        for step in range(REPS)
-        if side != 1 or step > 0
-    ]
-    for index, side, device, step in vector_moves:
-        target = lax.rem(rep + step, REPS)
+    for step, other in enumerate(others):
         copy = remote(
-            vectors_ref.at[target],
-            window_vectors_ref.at[side, rep],
-            vector_sems.at[0, index, step],
-            vector_sems.at[1, index, step],
-            (device, target),
+            vectors_ref.at[other],
+            window_vectors_ref.at[1, rep],
+            vector_sems.at[0, step],
+            vector_sems.at[1, step],
+            (leaf, other),
         )
         copy.start()
         sent.append(copy)
 
-    row_copies = []
+    side_copies = []
+
+    def pass_vectors():
+        for step, other in enumerate(others):
+            source = lax.rem(rep + REPS - 1 - step, REPS)
+            remote(
+                vectors_ref.at[rep],
+                window_vectors_ref.at[1, source],
+                vector_sems.at[0, step],
+                vector_sems.at[1, step],
+                (leaf, other),
+            ).wait_recv()
+        for index, (side, device) in enumerate(((2, before), (0, after))):
+            copy = remote(
+                window_vectors_ref.at[1],
+                window_vectors_ref.at[side],
+                vector_sems.at[0, REPS - 1 + index],
+                vector_sems.at[1, REPS - 1 + index],
+                (device, rep),
+            )
+            copy.start()
+            side_copies.append(copy)
+            sent.append(copy)
+
 
     def sort_points(k):
         number = k * REPS + rep
         points = choose(coordinate_slices(), order_of(order_ref, number))
         columns_ref[rep, k] = points.astype(BF16)
-        window_ref[1, k] = with_norms(points, False).T.astype(BF16)
-
-    def send_points(pair):
-        span = pl.ds(pair * 2, 2)
-        for index, (side, device) in enumerate(((2, before), (0, after))):
+
+    def send_points():
+        for index, (side, device) in enumerate(((1, before), (0, after))):
             copy = remote(
-                window_ref.at[1, span],
-                window_ref.at[side, span],
-                row_sems.at[0, pair, index],
-                row_sems.at[1, pair, index],
+                columns_ref.at[rep],
+                halo_ref.at[side],
+                row_sems.at[0, index],
+                row_sems.at[1, index],
                 (device, rep),
             )
             copy.start()
-            row_copies.append(copy)
+            side_copies.append(copy)
             sent.append(copy)
         for step, other in enumerate(others):
             copy = remote(
-                columns_ref.at[rep, span],
-                columns_ref.at[rep, span],
-                column_sems.at[0, pair, step],
-                column_sems.at[1, pair, step],
+                columns_ref.at[rep],
+                columns_ref.at[rep],
+                column_sems.at[0, step],
+                column_sems.at[1, step],
                 (leaf, other),
             )
             copy.start()
             sent.append(copy)
 
-    sort_points(0)
-    sort_points(1)
-    send_points(0)
+    for k in range(QUARTER):
+        sort_points(k)
+    send_points()
     push_finish(0)
     spread_finish(0)
-    sort_points(2)
-    sort_points(3)
-    send_points(1)
+    pass_vectors()
     push_finish(1)
     spread_finish(1)
     kernels(0, 5)
@@ -433,27 +445,16 @@
         running = coupling(level) + dot_wide_nt(running, top_ref[level, side])
     t_root_ref[...] = running
 
-    for copy in row_copies:
+    for copy in side_copies:
         copy.wait_recv()
-    for pair in range(2):
-        span = pl.ds(pair * 2, 2)
-        for step, other in enumerate(others):
-            source = lax.rem(rep + REPS - 1 - step, REPS)
-            remote(
-                columns_ref.at[rep, span],
-                columns_ref.at[source, span],
-                column_sems.at[0, pair, step],
-                column_sems.at[1, pair, step],
-                (leaf, other),
-            ).wait_recv()
-    for index, side, device, step in vector_moves:
-        source = lax.rem(rep + REPS - step, REPS)
+    for step, other in enumerate(others):
+        source = lax.rem(rep + REPS - 1 - step, REPS)
         remote(
-            vectors_ref.at[rep],
-            window_vectors_ref.at[side, source],
-            vector_sems.at[0, index, step],
-            vector_sems.at[1, index, step],
-            (device, lax.rem(rep + step, REPS)),
+            columns_ref.at[rep],
+            columns_ref.at[source],
+            column_sems.at[0, step],
+            column_sems.at[1, step],
+            (leaf, other),
         ).wait_recv()
     for copy in sent:
         copy.wait_send()
@@ -468,10 +469,11 @@
     window_vectors_ref,
     transfer_ref,
     basis_ref,
-    window_ref,
+    halo_ref,
     out_ref,
     own_out_ref,
     list_ref,
+    window_ref,
     own_ref,
     own_skel_ref,
     skel_rows_ref,
@@ -506,6 +508,13 @@
 
     lax.fori_loop(0, LEAVES, prepare, 0, unroll=4)
 
+    def partner_rows(k, _):
+        for side, points in enumerate((halo_ref[0, k], columns_ref[rep, k], halo_ref[1, k])):
+            window_ref[side * QUARTER + k] = with_norms(points.astype(F32), False).T.astype(BF16)
+        return 0
+
+    lax.fori_loop(0, QUARTER, partner_rows, 0, unroll=2)
+
     def from_root(leaf, _):
         t_ref[leaf, pl.ds(pl.multiple_of(rep * OWN, OWN), OWN), :] = fold_two(
             dot_nt(root_rows, transfer_ref[leaf])
@@ -625,7 +634,7 @@
         out_ref[:, :, leaf * LEAF : (leaf + 1) * LEAF] = jnp.concatenate([top, bottom], axis=1).astype(BF16)
 
 
-def combine_kernel(part_ref, own_ref, order_ref, out_ref, got_ref, sems):
+def combine_kernel(part_ref, own_ref, order_ref, out_ref, got_ref, marks_ref, sems):
     leaf = lax.axis_index("leaf")
     rep = lax.axis_index("rep")
     half = PTS // 2
@@ -634,20 +643,15 @@
     greet_signals(partners)
     greet_wait(partners)
     copies = []
-    for chunk in range(CHUNKS):
-        span = pl.ds(chunk * width, width)
-        for index, partner in enumerate(partners):
-            copy = remote(
-                part_ref.at[partner[1], :, span],
-                got_ref.at[index, :, span],
-                sems.at[0, index, chunk],
-                sems.at[1, index, chunk],
-                partner,
-            )
-            copy.start()
-            copies.append(copy)
+    for index, partner in enumerate(partners):
+        copy = remote(
+            part_ref.at[partner[1]], got_ref.at[index], sems.at[0, index], sems.at[1, index], partner
+        )
+        copy.start()
+        copies.append(copy)
 
     scattered = jnp.zeros((LEAVES * 2 * OWN, LEAF), F32)
+    highs = []
     for chunk in range(CHUNKS):
         here = [(number, (number * half + chunk * width) // LANES) for number in range(2)]
         positions = jnp.concatenate(
@@ -658,10 +662,13 @@
             ],
             axis=1,
         )
-        marks = one_hot(positions & 255)
-        high = jnp.broadcast_to(positions >> 8, (2 * OWN, 2 * width))
-        for copy in copies[chunk * len(partners) : (chunk + 1) * len(partners)]:
-            copy.wait_recv()
+        marks_ref[chunk] = one_hot(positions & 255)
+        highs.append(positions >> 8)
+    for copy in copies:
+        copy.wait()
+    for chunk in range(CHUNKS):
+        here = [(number, (number * half + chunk * width) // LANES) for number in range(2)]
+        high = jnp.broadcast_to(highs[chunk], (2 * OWN, 2 * width))
         totals = []
         for number, first in here:
             rows = slice(number * OWN, (number + 1) * OWN)
@@ -675,14 +682,12 @@
         rows = jnp.concatenate(
             [jnp.where(high == source, terms, 0.0).astype(BF16) for source in range(LEAVES)], axis=0
         )
-        scattered = scattered + dot_nt(rows, marks)
+        scattered = scattered + dot_nt(rows, marks_ref[chunk])
     for source in range(LEAVES):
         first = source * 2 * OWN
         out_ref[:, source * LEAF : (source + 1) * LEAF] = (
             scattered[first : first + OWN] + scattered[first + OWN : first + 2 * OWN]
         )
-    for copy in copies:
-        copy.wait_send()
 
 
 def vmem(count):
@@ -731,10 +736,10 @@
         right_sides.reshape(OWN, LEAVES, LEAF).transpose(1, 0, 2).reshape(LEAVES * OWN, LEAF),
         order,
     )
-    window, columns, window_vectors, t_root, times, skel_here = pl.pallas_call(
+    halo, columns, window_vectors, t_root, times, skel_here = pl.pallas_call(
         functools.partial(gather_kernel, count, levels),
         out_shape=(
-            shape((SIDES, QUARTER, LEAF, LANES), BF16),
+            shape((2, QUARTER, DIM, LEAF), BF16),
             shape((REPS, QUARTER, DIM, LEAF), BF16),
             shape((SIDES, REPS, 2 * OWN, 2 * LEAF), BF16),
             shape((OWN, RANK), F32),
@@ -753,9 +758,9 @@
         + [pltpu.VMEM((1 << width, OWN, RANK), F32) for _, width in spans]
         + [dma((2, 1 << width)) for _, width in spans]
         + [
-            dma((2, 2, 2)),
-            dma((2, 2, REPS - 1)),
-            dma((2, SIDES, REPS)),
+            dma((2, 2)),
+            dma((2, REPS - 1)),
+            dma((2, REPS + 1)),
             dma((2, levels, 1 << (max(PHASES) - 1))),
         ],
         compiler_params=params(0),
@@ -781,6 +786,7 @@
         out_specs=tuple(vmem(2)),
         scratch_shapes=[
             pltpu.SMEM((LEAVES * PARTNERS + 4 * WAYS + 8,), I32),
+            pltpu.VMEM((PARTNERS, LEAF, LANES), BF16),
             pltpu.VMEM((LEAVES, LANES, LEAF), BF16),
             pltpu.VMEM((LEAVES, LANES, RANK), BF16),
             pltpu.VMEM((QUARTER, RANK, LANES), BF16),
@@ -803,7 +809,7 @@
         window_vectors,
         leaf_transfer,
         leaf_basis,
-        window.reshape(PARTNERS, LEAF, LANES),
+        halo,
     )
 
     negative = pl.pallas_call(
@@ -813,7 +819,8 @@
         out_specs=pl.BlockSpec(memory_space=pltpu.VMEM),
         scratch_shapes=[
             pltpu.VMEM((REPS - 1, 2 * OWN, PTS // 2), BF16),
-            dma((2, REPS - 1, CHUNKS)),
+            pltpu.VMEM((CHUNKS, LEAF, PTS // CHUNKS), BF16),
+            dma((2, REPS - 1)),
         ],
         compiler_params=params(1),
         name="combine",

time: 55 us -> 54.7 us (level)
    pallas_call x1, Pallas kernels: 10.1 us -> 11.4 us  [on_device(): pl.pallas_call(near_kernel, out_shape=(shape((REPS, 2 * OWN, PTS // 2), B...]
    pallas_call x1, Pallas kernels: 10.5 us -> 9.49 us  [on_device(): pl.pallas_call(combine_kernel, out_shape=shape((OWN, PTS), F32), in_specs...]
where the time goes in v1:
time: 54.7 us; the launch traced here: 54.5 us
  Pallas kernels  51.6 us (94%)
  local copies, waits for them, and re-layouts  2.19 us (4%)
  other arithmetic  0.67 us (1%)
    pallas_call x1, Pallas kernels, on_device(): pl.pallas_call(functools.partial(gather_kernel, count, levels), out_shape...  29.7 us
    pallas_call x1, Pallas kernels, on_device(): pl.pallas_call(near_kernel, out_shape=(shape((REPS, 2 * OWN, PTS // 2), B...  11.4 us
    pallas_call x1, Pallas kernels, on_device(): pl.pallas_call(combine_kernel, out_shape=shape((OWN, PTS), F32), in_specs...  9.49 us
    unnamed x24, local copies, waits for them, and re-layouts  2.19 us

profile of v1, /device:TPU:2, one launch (start us, length us, event | category | flops | bytes accessed | tf_op | source)
XLA Modules:
  0.0 54.5 jit_solution(14987653350449287309)
XLA Ops:
  0.0 0.0 copy-start.4
  0.0 0.7 %copy-done.4 = s32[4096]{0:T(1024)S(1)} copy-done((s32[4096]{0:T(1024)S(1)}, s32[4096]{0:T(1024)}, u32[]{:S(2)}) %copy-start.4) | copy-done | bytes 16408
  0.7 0.0 copy-start.11
  0.7 0.8 %copy-done.11 = bf16[8,4096]{1,0:T(8,128)(2,1)S(1)} copy-done((bf16[8,4096]{1,0:T(8,128)(2,1)S(1)}, bf16[8,4096]{1,0:T(8,128)(2,1)}, u32[]{:S(2)}) %copy-start.11) | copy-done | bytes 65560
  1.6 0.0 copy-start
  1.6 0.0 copy-start.1
  1.6 0.0 copy-start.2
  1.6 0.0 copy-start.3
  1.6 0.0 copy-start.6
  1.6 0.0 copy-start.7
  1.6 0.0 copy-start.8
  1.6 0.0 copy-start.9
  1.6 0.0 copy-start.10
  1.6 1.0 %vectors.1.sorted_ref = f32[16,8,256]{2,1,0:T(8,128)S(1)} custom-call(bf16[128,256]{1,0:T(8,128)(2,1)S(1)} %bitcast.13, s32[32,128]{1,0:T(8,128)S(1)} %bitcast.8), custom_call_target="tpu_custom_call" | custom-call | flops 1000000000 | bytes 1000000 | tf_op jit(solution)/shard_map/vectors/pallas_call | solution.py:727
  2.6 0.2 copy-done
  2.8 0.1 copy-done.1
  2.9 0.2 copy-done.2
  3.1 0.1 copy-done.3
  3.2 0.0 copy-done.6
  3.2 0.0 copy-done.7
  3.2 0.0 copy-done.8
  3.2 0.0 copy-done.9
  3.2 0.0 copy-done.10
  3.2 29.7 %gather.1 = (bf16[2,4,64,256]{3,2,1,0:T(8,128)(2,1)S(1)}, bf16[4,4,64,256]{3,2,1,0:T(8,128)(2,1)S(1)}, bf16[3,4,16,512]{3,2,1,0:T(8,128)(2,1)S(1)}, f32[8,128]{1...) custom-call(bf16[64,4096]{1,0:T(8,128)(2,1)S(1)} %copy-done.2, f32[16,8,256]{2,1,0:T(8,128)S(1)} %vectors.1.sorted_ref, ...), custom_call_target="tpu_custom_call" | custom-call | tf_op jit(solution)/shard_map/gather/pallas_call | solution.py:739
  32.9 0.0 copy-start.5
  32.9 11.4 %near.1 = (bf16[4,16,2048]{2,1,0:T(8,128)(2,1)S(1)}, f32[8,4096]{1,0:T(8,128)S(1)}) custom-call(s32[16,128]{1,0:T(8,128)S(1)} %get-tuple-element.13.times_ref, bf16[4,4,64,256]{3,2,1,0:T(8,128)(2,1)S(1)} %get-tuple-element.14.columns_ref, s32[16,128]{1,0:T(8,128)S(1)} %get-tuple-element.15.skel_leaf_ref, f32[8,128]{1,0:T(8,128)S(1)} %get-tuple-element.16.t_root_ref, ...), custom_call_target="tpu_custom_call" | custom-call | tf_op jit(solution)/shard_map/near/pallas_call | solution.py:782
  44.3 0.0 copy-done.5
  44.3 9.5 %combine.1 = f32[8,4096]{1,0:T(8,128)S(1)} custom-call(bf16[4,16,2048]{2,1,0:T(8,128)(2,1)S(1)} %get-tuple-element.19.part_ref, f32[8,4096]{1,0:T(8,128)S(1)} %get-tuple-element.20.own_ref, s32[32,128]{1,0:T(8,128)S(1)} %bitcast.10), custom_call_target="tpu_custom_call" | custom-call | tf_op jit(solution)/shard_map/combine/pallas_call | solution.py:815
  53.8 0.7 %neg.3 = f32[8,4096]{1,0:T(8,128)} negate(f32[8,4096]{1,0:T(8,128)S(1)} %combine.1) | non-fusion elementwise | flops 32768 | bytes 262144 | tf_op jit(solution)/shard_map/neg | solution.py:828
Async XLA Ops:
  0.0 0.7 %copy-start.4 = (s32[4096]{0:T(1024)S(1)}, s32[4096]{0:T(1024)}, u32[]{:S(2)}) copy-start(s32[4096]{0:T(1024)} %param.13) | copy-start | bytes 49156
  0.7 0.8 %copy-start.11 = (bf16[8,4096]{1,0:T(8,128)(2,1)S(1)}, bf16[8,4096]{1,0:T(8,128)(2,1)}, u32[]{:S(2)}) copy-start(bf16[8,4096]{1,0:T(8,128)(2,1)} %param.12) | copy-start | bytes 196612
  1.6 1.2 %copy-start = (bf16[16,256,128]{2,1,0:T(8,128)(2,1)S(1)}, bf16[16,256,128]{2,1,0:T(8,128)(2,1)}, u32[]{:S(2)}) copy-start(bf16[16,256,128]{2,1,0:T(8,128)(2,1)} %basis_ref.3) | copy-start | bytes 3145732
  1.6 1.4 %copy-start.1 = (bf16[16,128,128]{2,1,0:T(8,128)(2,1)S(1)}, bf16[16,128,128]{2,1,0:T(8,128)(2,1)}, u32[]{:S(2)}) copy-start(bf16[16,128,128]{2,1,0:T(8,128)(2,1)} %transfer_ref.3) | copy-start | bytes 1572868
  1.6 1.5 %copy-start.2 = (bf16[64,4096]{1,0:T(8,128)(2,1)S(1)}, bf16[64,4096]{1,0:T(8,128)(2,1)}, u32[]{:S(2)}) copy-start(bf16[64,4096]{1,0:T(8,128)(2,1)} %coords_ref.1) | copy-start | bytes 1572868
  1.6 1.6 %copy-start.3 = (bf16[6,2,128,128]{3,2,1,0:T(8,128)(2,1)S(1)}, bf16[6,2,128,128]{3,2,1,0:T(8,128)(2,1)}, u32[]{:S(2)}) copy-start(bf16[6,2,128,128]{3,2,1,0:T(8,128)(2,1)} %top_ref.1) | copy-start | bytes 1179652
  1.6 1.6 %copy-start.6 = (s32[16,128]{1,0:T(8,128)S(1)}, s32[16,128]{1,0:T(8,128)}, u32[]{:S(2)}) copy-start(s32[16,128]{1,0:T(8,128)} %skel_leaf_ref.1) | copy-start | bytes 24580
  1.6 1.6 %copy-start.7 = (s32[16,24]{1,0:T(8,128)S(1)}, s32[16,24]{1,0:T(8,128)}, u32[]{:S(2)}) copy-start(s32[16,24]{1,0:T(8,128)} %near_ref.1) | copy-start | bytes 4612
  1.6 1.6 %copy-start.8 = (s32[16,8]{0,1:T(8,128)S(1)}, s32[16,8]{0,1:T(8,128)}, u32[]{:S(2)}) copy-start(s32[16,8]{0,1:T(8,128)} %param.19) | copy-start | bytes 1540
  1.6 1.6 %copy-start.9 = (s32[1,128]{1,0:T(1,128)S(1)}, s32[1,128]{1,0:T(1,128)}, u32[]{:S(2)}) copy-start(s32[1,128]{1,0:T(1,128)} %skel_root_ref.1) | copy-start | bytes 1540
  1.6 1.6 %copy-start.10 = (s32[16]{0:T(128)S(1)}, s32[16]{0:T(128)}, u32[]{:S(2)}) copy-start(s32[16]{0:T(128)} %param.21) | copy-start | bytes 196
  32.9 11.4 %copy-start.5 = (s32[4096]{0:T(1024)S(1)}, s32[4096]{0:T(1024)}, u32[]{:S(2)}) copy-start(s32[4096]{0:T(1024)} %param.13) | copy-start | bytes 49156

commit v2 on v1

--- a/solution.py
+++ b/solution.py
@@ -378,7 +378,7 @@
         points = choose(coordinate_slices(), order_of(order_ref, number))
         columns_ref[rep, k] = points.astype(BF16)
 
-    def send_points():
+    def send_sides():
         for index, (side, device) in enumerate(((1, before), (0, after))):
             copy = remote(
                 columns_ref.at[rep],
@@ -390,6 +390,8 @@
             copy.start()
             side_copies.append(copy)
             sent.append(copy)
+
+    def send_columns():
         for step, other in enumerate(others):
             copy = remote(
                 columns_ref.at[rep],
@@ -403,12 +405,13 @@
 
     for k in range(QUARTER):
         sort_points(k)
-    send_points()
+    send_columns()
     push_finish(0)
     spread_finish(0)
-    pass_vectors()
     push_finish(1)
     spread_finish(1)
+    send_sides()
+    pass_vectors()
     kernels(0, 5)
     push_finish(2)
     kernels(5, 7)
@@ -437,12 +440,22 @@
     times_ref[...] = times.astype(I32)
     skel_out_ref[...] = skel_leaf_ref[...]
 
+    split = spans[-1][0]
+    sides = [lax.rem(leaf // (1 << level), 2) for level in range(levels)]
+    lower = coupling(split - 1)
+    for level in range(split - 2, -1, -1):
+        lower = coupling(level) + dot_wide_nt(lower, top_ref[level, sides[level]])
+    product = top_ref[0, sides[0]].astype(F32)
+    for level in range(1, split):
+        product = dot_wide(product, top_ref[level, sides[level]])
+    product_high, product_low = split_two(product)
+
     spread_finish(2)
-
     running = coupling(levels - 1)
-    for level in range(levels - 2, -1, -1):
-        side = lax.rem(leaf // (1 << level), 2)
-        running = coupling(level) + dot_wide_nt(running, top_ref[level, side])
+    for level in range(levels - 2, split - 1, -1):
+        running = coupling(level) + dot_wide_nt(running, top_ref[level, sides[level]])
+    rows = stack_two(running)
+    running = lower + (fold_two(dot_nt(rows, product_high)) + fold_two(dot_nt(rows, product_low)))
     t_root_ref[...] = running
 
     for copy in side_copies:

time: 54.7 us -> 56.8 us (1.038)
  the two profiles are of different devices: /device:TPU:2 before, /device:TPU:8 now
where the time goes in v2:
time: 56.8 us; the launch traced here: 56.5 us
  Pallas kernels  53.6 us (94%)
  local copies, waits for them, and re-layouts  2.18 us (4%)
  other arithmetic  0.67 us (1%)
    pallas_call x1, Pallas kernels, on_device(): pl.pallas_call(functools.partial(gather_kernel, count, levels), out_shape...  33.6 us
    pallas_call x1, Pallas kernels, on_device(): pl.pallas_call(near_kernel, out_shape=(shape((REPS, 2 * OWN, PTS // 2), B...  11.7 us
    pallas_call x1, Pallas kernels, on_device(): pl.pallas_call(combine_kernel, out_shape=shape((OWN, PTS), F32), in_specs...  7.3 us
    unnamed x24, local copies, waits for them, and re-layouts  2.18 us

profile of v2, /device:TPU:8, one launch (start us, length us, event | category | flops | bytes accessed | tf_op | source)
XLA Modules:
  0.0 56.5 jit_solution(12440580464146958555)
XLA Ops:
  0.0 0.0 copy-start.4
  0.0 0.7 %copy-done.4 = s32[4096]{0:T(1024)S(1)} copy-done((s32[4096]{0:T(1024)S(1)}, s32[4096]{0:T(1024)}, u32[]{:S(2)}) %copy-start.4) | copy-done | bytes 16408
  0.7 0.0 copy-start.11
  0.7 0.8 %copy-done.11 = bf16[8,4096]{1,0:T(8,128)(2,1)S(1)} copy-done((bf16[8,4096]{1,0:T(8,128)(2,1)S(1)}, bf16[8,4096]{1,0:T(8,128)(2,1)}, u32[]{:S(2)}) %copy-start.11) | copy-done | bytes 65560
  1.6 0.0 copy-start
  1.6 0.0 copy-start.1
  1.6 0.0 copy-start.2
  1.6 0.0 copy-start.3
  1.6 0.0 copy-start.6
  1.6 0.0 copy-start.7
  1.6 0.0 copy-start.8
  1.6 0.0 copy-start.9
  1.6 0.0 copy-start.10
  1.6 1.0 %vectors.1.sorted_ref = f32[16,8,256]{2,1,0:T(8,128)S(1)} custom-call(bf16[128,256]{1,0:T(8,128)(2,1)S(1)} %bitcast.13, s32[32,128]{1,0:T(8,128)S(1)} %bitcast.8), custom_call_target="tpu_custom_call" | custom-call | flops 1000000000 | bytes 1000000 | tf_op jit(solution)/shard_map/vectors/pallas_call | solution.py:740
  2.6 0.2 copy-done
  2.8 0.1 copy-done.1
  2.9 0.2 copy-done.2
  3.1 0.1 copy-done.3
  3.2 0.0 copy-done.6
  3.2 0.0 copy-done.7
  3.2 0.0 copy-done.8
  3.2 0.0 copy-done.9
  3.2 0.0 copy-done.10
  3.2 33.6 %gather.1 = (bf16[2,4,64,256]{3,2,1,0:T(8,128)(2,1)S(1)}, bf16[4,4,64,256]{3,2,1,0:T(8,128)(2,1)S(1)}, bf16[3,4,16,512]{3,2,1,0:T(8,128)(2,1)S(1)}, f32[8,128]{1...) custom-call(bf16[64,4096]{1,0:T(8,128)(2,1)S(1)} %copy-done.2, f32[16,8,256]{2,1,0:T(8,128)S(1)} %vectors.1.sorted_ref, ...), custom_call_target="tpu_custom_call" | custom-call | tf_op jit(solution)/shard_map/gather/pallas_call | solution.py:752
  36.9 0.0 copy-start.5
  36.9 11.7 %near.1 = (bf16[4,16,2048]{2,1,0:T(8,128)(2,1)S(1)}, f32[8,4096]{1,0:T(8,128)S(1)}) custom-call(s32[16,128]{1,0:T(8,128)S(1)} %get-tuple-element.13.times_ref, bf16[4,4,64,256]{3,2,1,0:T(8,128)(2,1)S(1)} %get-tuple-element.14.columns_ref, s32[16,128]{1,0:T(8,128)S(1)} %get-tuple-element.15.skel_leaf_ref, f32[8,128]{1,0:T(8,128)S(1)} %get-tuple-element.16.t_root_ref, ...), custom_call_target="tpu_custom_call" | custom-call | tf_op jit(solution)/shard_map/near/pallas_call | solution.py:795
  48.6 0.0 copy-done.5
  48.6 7.3 %combine.1 = f32[8,4096]{1,0:T(8,128)S(1)} custom-call(bf16[4,16,2048]{2,1,0:T(8,128)(2,1)S(1)} %get-tuple-element.19.part_ref, f32[8,4096]{1,0:T(8,128)S(1)} %get-tuple-element.20.own_ref, s32[32,128]{1,0:T(8,128)S(1)} %bitcast.10), custom_call_target="tpu_custom_call" | custom-call | tf_op jit(solution)/shard_map/combine/pallas_call | solution.py:828
  55.9 0.7 %neg.3 = f32[8,4096]{1,0:T(8,128)} negate(f32[8,4096]{1,0:T(8,128)S(1)} %combine.1) | non-fusion elementwise | flops 32768 | bytes 262144 | tf_op jit(solution)/shard_map/neg | solution.py:841
Async XLA Ops:
  0.0 0.7 %copy-start.4 = (s32[4096]{0:T(1024)S(1)}, s32[4096]{0:T(1024)}, u32[]{:S(2)}) copy-start(s32[4096]{0:T(1024)} %param.13) | copy-start | bytes 49156
  0.7 0.8 %copy-start.11 = (bf16[8,4096]{1,0:T(8,128)(2,1)S(1)}, bf16[8,4096]{1,0:T(8,128)(2,1)}, u32[]{:S(2)}) copy-start(bf16[8,4096]{1,0:T(8,128)(2,1)} %param.12) | copy-start | bytes 196612
  1.6 1.2 %copy-start = (bf16[16,256,128]{2,1,0:T(8,128)(2,1)S(1)}, bf16[16,256,128]{2,1,0:T(8,128)(2,1)}, u32[]{:S(2)}) copy-start(bf16[16,256,128]{2,1,0:T(8,128)(2,1)} %basis_ref.3) | copy-start | bytes 3145732
  1.6 1.4 %copy-start.1 = (bf16[16,128,128]{2,1,0:T(8,128)(2,1)S(1)}, bf16[16,128,128]{2,1,0:T(8,128)(2,1)}, u32[]{:S(2)}) copy-start(bf16[16,128,128]{2,1,0:T(8,128)(2,1)} %transfer_ref.3) | copy-start | bytes 1572868
  1.6 1.5 %copy-start.2 = (bf16[64,4096]{1,0:T(8,128)(2,1)S(1)}, bf16[64,4096]{1,0:T(8,128)(2,1)}, u32[]{:S(2)}) copy-start(bf16[64,4096]{1,0:T(8,128)(2,1)} %coords_ref.1) | copy-start | bytes 1572868
  1.6 1.6 %copy-start.3 = (bf16[6,2,128,128]{3,2,1,0:T(8,128)(2,1)S(1)}, bf16[6,2,128,128]{3,2,1,0:T(8,128)(2,1)}, u32[]{:S(2)}) copy-start(bf16[6,2,128,128]{3,2,1,0:T(8,128)(2,1)} %top_ref.1) | copy-start | bytes 1179652
  1.6 1.6 %copy-start.6 = (s32[16,128]{1,0:T(8,128)S(1)}, s32[16,128]{1,0:T(8,128)}, u32[]{:S(2)}) copy-start(s32[16,128]{1,0:T(8,128)} %skel_leaf_ref.1) | copy-start | bytes 24580
  1.6 1.6 %copy-start.7 = (s32[16,24]{1,0:T(8,128)S(1)}, s32[16,24]{1,0:T(8,128)}, u32[]{:S(2)}) copy-start(s32[16,24]{1,0:T(8,128)} %near_ref.1) | copy-start | bytes 4612
  1.6 1.6 %copy-start.8 = (s32[16,8]{0,1:T(8,128)S(1)}, s32[16,8]{0,1:T(8,128)}, u32[]{:S(2)}) copy-start(s32[16,8]{0,1:T(8,128)} %param.19) | copy-start | bytes 1540
  1.6 1.6 %copy-start.9 = (s32[1,128]{1,0:T(1,128)S(1)}, s32[1,128]{1,0:T(1,128)}, u32[]{:S(2)}) copy-start(s32[1,128]{1,0:T(1,128)} %skel_root_ref.1) | copy-start | bytes 1540
  1.6 1.6 %copy-start.10 = (s32[16]{0:T(128)S(1)}, s32[16]{0:T(128)}, u32[]{:S(2)}) copy-start(s32[16]{0:T(128)} %param.21) | copy-start | bytes 196
  36.9 11.7 %copy-start.5 = (s32[4096]{0:T(1024)S(1)}, s32[4096]{0:T(1024)}, u32[]{:S(2)}) copy-start(s32[4096]{0:T(1024)} %param.13) | copy-start | bytes 49156
